TPU v7x, 32 devices: a whole 2x2x4 slice. The times are simulated.
32 devices in a mesh: row: 4 (over z), sector: 8 (over y, x, core).
Axes of the slice: x: 2, y: 2, z: 4, core: 2. Of those that a mesh axis runs over, the one named last changes fastest.
Arguments:
- boundary_in: float32 [8, 128, 256], P('sector'), may hold values from -6 to 6
- left_transfer: float32 [4, 8, 128, 128], P('row', 'sector'), may hold values from -0.25 to 0.25
- right_transfer: float32 [4, 256, 256], P('row'), may hold values from -0.36 to 0.36
- env_weight: bfloat16 [4, 4, 256, 256], P('row'), may hold values from -50000 to 50000
- ranks: int32 [8], P('sector'), may hold values from 32 to 128, as said below
- routes: int32 [8, 4], P('sector'), may hold values from 0 to 7, all different within a row; in each aligned block of 8 rows (0 to 7, 8 to 15, ...) at most 6 rows name the same one
- owner: int32 [8], replicated, may hold values from 0 to 7, each once
Outputs:
- boundary_out: float32 [4, 8, 128, 256], P('row', 'sector')
- environment: float32 [4, 8, 128, 256], P('row', 'sector')
Inputs may be any that keep to these rules, and one draw needn't show every extreme that they name: `ranks`: at least one sector has rank 128. `routes`: each row names 4 different sectors; no sector is named by more than 6 rows. `owner`: each sector index once.
All inputs are finite; a program needn't handle non-finite values.
Results may differ from a plain program's by a relative error of at most 0.013.
Values may be sent and summed in bfloat16 or wider, within the bound.
A program may use at most 64 MiB of HBM per device.

v0:
```python
import jax
import jax.numpy as jnp
from jax import lax
from jax.sharding import PartitionSpec as P


def passed_along(value, axis, steps):
    count = lax.axis_size(axis)
    leading, last = (max(0, -steps), min(count, count - steps))
    return lax.ppermute(value, axis, [(source, source + steps) for source in range(leading, last)])


def on_device(boundary_in, left_transfer, right_transfer, env_weight, ranks, routes, owner):
    highest = lax.Precision.HIGHEST
    block_size = boundary_in.shape[1]
    pair_size = boundary_in.shape[2]
    sector_count = owner.shape[0]
    kept_rows = (jnp.arange(block_size) < ranks[0]).astype(jnp.float32)
    initial = boundary_in[0] * kept_rows[:, None]
    unit_block = jnp.eye(block_size, dtype=jnp.float32)
    unit_pairs = jnp.eye(pair_size, dtype=jnp.float32)
    left_op = kept_rows[:, None] * (0.9 * unit_block + left_transfer[0, 0]) * kept_rows[None, :]
    right_op = 0.9 * unit_pairs + right_transfer[0]

    def absorb(matrix):
        inner = jnp.dot(left_op, matrix, precision=highest, preferred_element_type=jnp.float32)
        return jnp.dot(inner, right_op, precision=highest, preferred_element_type=jnp.float32)

    row_position = lax.axis_index("row")

    def advance(turn, carried):
        previous = passed_along(carried, "row", 1)
        previous = jnp.where(row_position == 0, initial, previous)
        return absorb(previous)

    current = lax.fori_loop(0, lax.axis_size("row") - 1, advance, absorb(initial))
    rounded = current.astype(jnp.bfloat16)
    partials = jnp.einsum(
        "ab,jbc->jac", rounded, env_weight[0], preferred_element_type=jnp.float32
    ).astype(jnp.bfloat16)
    sector_ids = jnp.arange(sector_count)
    matches = (routes[0][:, None] == sector_ids[None, :]).astype(jnp.int32)
    target_owner = jnp.sum(matches * owner[None, :], axis=1)
    selector = (target_owner[None, :] == sector_ids[:, None]).astype(jnp.bfloat16)
    owner_terms = jnp.einsum("oj,jac->oac", selector, partials, preferred_element_type=jnp.float32)
    blocks = owner_terms.astype(jnp.bfloat16)
    arrived = lax.all_to_all(blocks, "sector", split_axis=0, concat_axis=0, tiled=True)
    environment = jnp.sum(arrived.astype(jnp.float32), axis=0, keepdims=True)
    return (current[None, None], environment[None])


def solution(mesh):
    return jax.shard_map(
        on_device,
        mesh=mesh,
        in_specs=(
            P("sector", None, None),
            P("row", "sector", None, None),
            P("row", None, None),
            P("row", None, None, None),
            P("sector"),
            P("sector", None),
            P(),
        ),
        out_specs=(P("row", "sector", None, None), P("row", "sector", None, None)),
        check_vma=False,
    )
```

profile of v0, /device:TPU:0, one launch (start us, length us, event | category | flops | bytes accessed | tf_op | source)
XLA Modules:
  0.0 43.6 jit_solution(5257731657595675897)
XLA Ops:
  1.4 1.0 %fusion.11 = f32[128,128]{1,0:T(8,128)S(1)} fusion(f32[1,1,128,128]{3,2,1,0:T(8,128)} %param.10, f32[128]{0:T(128)S(1)} %compare_convert_fusion), kind=kLoop, calls=%fused_computation.18 | loop fusion | flops 81920 | bytes 131584 | tf_op jit(solution)/shard_map/mul | solution.py:22
  2.5 0.3 fusion.6
  2.9 0.5 %copy-done.1 = f32[1,256,256]{2,1,0:T(8,128)S(1)} copy-done((f32[1,256,256]{2,1,0:T(8,128)S(1)}, f32[1,256,256]{2,1,0:T(8,128)}, u32[]{:S(2)}) %copy-start.1) | copy-done | bytes 262168
  3.4 0.3 fusion.28
  3.7 0.6 %copy-done.5 = s32[8]{0:T(128)S(1)} copy-done((s32[8]{0:T(128)S(1)}, s32[8]{0:T(128)}, u32[]{:S(2)}) %copy-start.5) | copy-done | bytes 56
  4.4 0.2 select_reduce_fusion
  4.5 23.9 %while.12 = (s32[]{:T(128)}, f32[128,256]{1,0:T(8,128)S(1)}, pred[]{:T(512)}, f32[128,256]{1,0:T(8,128)S(1)}, f32[128,128]{1,0:T(8,128)S(1)}, /*index=5*/f32[256,256]{1,0:T(8,128)S(1)}, s32[]{:T(128)}) while((s32[]{:T(128)}, f32[128,256]{1,0:T(8,128)S(1)}, pred[]{:T(512)}, f32[128,256]{1,0:T(8,128)S(1)}, f32[128,128]{1,0:T(8,128)S(1)}, ...), condition=%wide.region_1.2_spmd, body=%wide.region_0.1_spmd.sunk | while | flops 151027712 | bytes 1507446 | solution.py:36
  4.6 4.9 %collective-permute-start = (f32[128,256]{1,0:T(8,128)S(1)}, f32[128,256]{1,0:T(8,128)S(1)}, u32[]{:S(2)}, u32[]{:S(2)}) collective-permute-start(f32[128,256]{1,0:T(8,128)S(1)} %get-tuple-element.132), channel_id=1, source_target_pairs={{0,8},{8,16},{16,24},{1,9},{9,17},{17,25},{2,10},{10,18},{18,26},{... | collective-permute-start | bytes 393224 | tf_op jit(solution)/shard_map/while/body/eval_jaxpr/ppermute | solution.py:10
  9.5 2.7 %collective-permute-done = f32[128,256]{1,0:T(8,128)S(1)} collective-permute-done((f32[128,256]{1,0:T(8,128)S(1)}, f32[128,256]{1,0:T(8,128)S(1)}, u32[]{:S(2)}, u32[]{:S(2)}) %collective-permute-start) | collective-permute-done | bytes 131104 | tf_op jit(solution)/shard_map/while/body/eval_jaxpr/ppermute | solution.py:10
  12.2 0.4 fusion.44
  12.6 0.4 fusion.45
  13.0 4.4 %collective-permute-start = (f32[128,256]{1,0:T(8,128)S(1)}, f32[128,256]{1,0:T(8,128)S(1)}, u32[]{:S(2)}, u32[]{:S(2)}) collective-permute-start(f32[128,256]{1,0:T(8,128)S(1)} %get-tuple-element.132), channel_id=1, source_target_pairs={{0,8},{8,16},{16,24},{1,9},{9,17},{17,25},{2,10},{10,18},{18,26},{... | collective-permute-start | bytes 393224 | tf_op jit(solution)/shard_map/while/body/eval_jaxpr/ppermute | solution.py:10
  17.4 2.5 %collective-permute-done = f32[128,256]{1,0:T(8,128)S(1)} collective-permute-done((f32[128,256]{1,0:T(8,128)S(1)}, f32[128,256]{1,0:T(8,128)S(1)}, u32[]{:S(2)}, u32[]{:S(2)}) %collective-permute-start) | collective-permute-done | bytes 131104 | tf_op jit(solution)/shard_map/while/body/eval_jaxpr/ppermute | solution.py:10
  19.9 0.4 fusion.44
  20.3 0.4 fusion.45
  20.7 4.4 %collective-permute-start = (f32[128,256]{1,0:T(8,128)S(1)}, f32[128,256]{1,0:T(8,128)S(1)}, u32[]{:S(2)}, u32[]{:S(2)}) collective-permute-start(f32[128,256]{1,0:T(8,128)S(1)} %get-tuple-element.132), channel_id=1, source_target_pairs={{0,8},{8,16},{16,24},{1,9},{9,17},{17,25},{2,10},{10,18},{18,26},{... | collective-permute-start | bytes 393224 | tf_op jit(solution)/shard_map/while/body/eval_jaxpr/ppermute | solution.py:10
  25.1 2.5 %collective-permute-done = f32[128,256]{1,0:T(8,128)S(1)} collective-permute-done((f32[128,256]{1,0:T(8,128)S(1)}, f32[128,256]{1,0:T(8,128)S(1)}, u32[]{:S(2)}, u32[]{:S(2)}) %collective-permute-start) | collective-permute-done | bytes 131104 | tf_op jit(solution)/shard_map/while/body/eval_jaxpr/ppermute | solution.py:10
  27.6 0.4 fusion.44
  28.0 0.4 fusion.45
  28.4 0.2 fusion.3
  28.7 0.4 copy-done.3
  29.1 0.4 convolution_convert_fusion
  29.6 13.3 %all_to_all.5 = bf16[8,128,256]{2,1,0:T(8,128)(2,1)S(1)} all-to-all(bf16[8,128,256]{2,1,0:T(8,128)(2,1)S(1)} %copy.11), channel_id=1, replica_groups=mesh['row'=4,'sector'=8] {'sector'}, dimensions={0} | all-to-all | bytes 1048576 | tf_op jit(solution)/shard_map/all_to_all | solution.py:47
  42.9 0.7 %convert_reduce_fusion = f32[128,256]{1,0:T(8,128)} fusion(bf16[8,128,256]{2,1,0:T(8,128)(2,1)S(1)} %all_to_all.5), kind=kLoop, calls=%fused_computation.6 | loop fusion | flops 491520 | bytes 655360 | tf_op jit(solution)/shard_map/reduce_sum | solution.py:48
  (15 shorter events, 0.3 us)
Async XLA Ops:
  0.6 27.8 %copy-start = (bf16[1,4,256,256]{3,2,1,0:T(8,128)(2,1)S(1)}, bf16[1,4,256,256]{3,2,1,0:T(8,128)(2,1)}, u32[]{:S(2)}) copy-start(bf16[1,4,256,256]{3,2,1,0:T(8,128)(2,1)} %param.12) | copy-start | bytes 1572868
  0.6 1.7 %copy-start.2 = (f32[1,128,256]{2,1,0:T(8,128)S(1)}, f32[1,128,256]{2,1,0:T(8,128)}, u32[]{:S(2)}) copy-start(f32[1,128,256]{2,1,0:T(8,128)} %param.9) | copy-start | bytes 393220
  1.4 1.1 %copy-start.4 = (f32[1,1,128,128]{3,2,1,0:T(8,128)S(1)}, f32[1,1,128,128]{3,2,1,0:T(8,128)}, u32[]{:S(2)}) copy-start(f32[1,1,128,128]{3,2,1,0:T(8,128)} %param.10) | copy-start | bytes 196612
  2.4 1.0 %copy-start.1 = (f32[1,256,256]{2,1,0:T(8,128)S(1)}, f32[1,256,256]{2,1,0:T(8,128)}, u32[]{:S(2)}) copy-start(f32[1,256,256]{2,1,0:T(8,128)} %param.11) | copy-start | bytes 786436
  3.7 0.7 %copy-start.5 = (s32[8]{0:T(128)S(1)}, s32[8]{0:T(128)}, u32[]{:S(2)}) copy-start(s32[8]{0:T(128)} %param.15) | copy-start | bytes 100
  3.7 0.7 %copy-start.6 = (s32[1,4]{1,0:T(1,128)S(1)}, s32[1,4]{1,0:T(1,128)}, u32[]{:S(2)}) copy-start(s32[1,4]{1,0:T(1,128)} %param.14) | copy-start | bytes 52
  4.6 7.7 %collective-permute-start = (f32[128,256]{1,0:T(8,128)S(1)}, f32[128,256]{1,0:T(8,128)S(1)}, u32[]{:S(2)}, u32[]{:S(2)}) collective-permute-start(f32[128,256]{1,0:T(8,128)S(1)} %get-tuple-element.132), channel_id=1, source_target_pairs={{0,8},{8,16},{16,24},{1,9},{9,17},{17,25},{2,10},{10,18},{18,26},{... | collective-permute-start | bytes 393224 | tf_op jit(solution)/shard_map/while/body/eval_jaxpr/ppermute | solution.py:10
  13.0 6.9 %collective-permute-start = (f32[128,256]{1,0:T(8,128)S(1)}, f32[128,256]{1,0:T(8,128)S(1)}, u32[]{:S(2)}, u32[]{:S(2)}) collective-permute-start(f32[128,256]{1,0:T(8,128)S(1)} %get-tuple-element.132), channel_id=1, source_target_pairs={{0,8},{8,16},{16,24},{1,9},{9,17},{17,25},{2,10},{10,18},{18,26},{... | collective-permute-start | bytes 393224 | tf_op jit(solution)/shard_map/while/body/eval_jaxpr/ppermute | solution.py:10
  20.7 6.9 %collective-permute-start = (f32[128,256]{1,0:T(8,128)S(1)}, f32[128,256]{1,0:T(8,128)S(1)}, u32[]{:S(2)}, u32[]{:S(2)}) collective-permute-start(f32[128,256]{1,0:T(8,128)S(1)} %get-tuple-element.132), channel_id=1, source_target_pairs={{0,8},{8,16},{16,24},{1,9},{9,17},{17,25},{2,10},{10,18},{18,26},{... | collective-permute-start | bytes 393224 | tf_op jit(solution)/shard_map/while/body/eval_jaxpr/ppermute | solution.py:10
  28.4 0.7 %copy-start.3 = (f32[128,256]{1,0:T(8,128)}, f32[128,256]{1,0:T(8,128)S(1)}, u32[]{:S(2)}) copy-start(f32[128,256]{1,0:T(8,128)S(1)} %get-tuple-element.74) | copy-start | bytes 393220
where the time goes:
time: 43.9 us; the launch traced here: 43.6 us
  starting transfers between devices  13.7 us (31%)
  blocking collectives  13.3 us (30%)
  waiting for transfers between devices  7.72 us (18%)
  matrix products  3.63 us (8%)
  other arithmetic  2 us (5%)
  local copies, waits for them, and re-layouts  1.68 us (4%)
  between operations  1.51 us (3%)
    ppermute x3, starting transfers between devices, passed_along(): lax.ppermute(value, axis, [(source, source + steps) for source in range(l...  13.7 us
    all_to_all x1, blocking collectives, on_device(): lax.all_to_all(blocks, 'sector', split_axis=0, concat_axis=0, tiled=True)  13.3 us
    ppermute x3, waiting for transfers between devices, passed_along(): lax.ppermute(value, axis, [(source, source + steps) for source in range(l...  7.72 us
    unnamed x14, local copies, waits for them, and re-layouts  1.58 us
    dot_general x4, matrix products, absorb(): jnp.dot(left_op, matrix, precision=highest, preferred_element_type=jnp.fl...  1.49 us
    dot_general x4, matrix products, absorb(): jnp.dot(inner, right_op, precision=highest, preferred_element_type=jnp.fl...  1.48 us
    mul x1, other arithmetic, on_device(): kept_rows[:, None] * (0.9 * unit_block + left_transfer[0, 0])  0.99 us
  transfers between devices with their start and end apart: 3, of which 3 were waited for; matrix products, arithmetic and copies ran while one was open for 0% of the time, Pallas kernels for 0%

commit v1 on v0

v1 whole, which is shorter than its diff:
```python
import functools

import jax
import jax.numpy as jnp
from jax import lax
from jax.experimental import pallas as pl
from jax.experimental.pallas import tpu as pltpu
from jax.sharding import PartitionSpec as P

MESH = pl.DeviceIdType.MESH
BF16 = jnp.bfloat16
F32 = jnp.float32


def partner(index, step, count):
    if count & (count - 1):
        return lax.rem(index + step, count), lax.rem(index - step + count, count)
    result, bit = 0, 1
    while bit < count:
        own = lax.rem(index // bit, 2)
        result = result + ((1 - own) if step & bit else own) * bit
        bit *= 2
    return result, result


def kernel(
    rows, sectors, slices,
    ranks, routes, owner, boundary_in, left, right, weight,
    bound_out, env_out,
    left_bf, left_in, right_bf, y_f32, chain_in, pairs, ys, info, chosen,
    left_send, left_recv, chain_send, chain_recv, pair_send, pair_recv,
    y_send, y_recv, twin_send, info_send, info_recv,
):
    row, sector = lax.axis_index("row"), lax.axis_index("sector")
    slots = weight.shape[1]
    block, width = boundary_in.shape[1], boundary_in.shape[2]
    piece_rows = width // slices
    piece = lax.rem(sector, slices)
    group_base = sector - piece
    groups = sectors // 2
    group, core = sector // 2, lax.rem(sector, 2)
    twin = group * 2 + 1 - core

    barrier = pltpu.get_barrier_semaphore()
    for step in range(1, rows):
        pl.semaphore_signal(barrier, inc=1, device_id=(lax.rem(row + step, rows), sector), device_id_type=MESH)
    for step in range(1, sectors):
        pl.semaphore_signal(barrier, inc=1, device_id=(row, lax.rem(sector + step, sectors)), device_id_type=MESH)

    left_bf[...] = left[0, 0].astype(BF16)
    right_bf[...] = right[0].astype(BF16)
    for j in range(slots):
        info[sector, pl.ds(j, 1), :] = jnp.full((1, 128), owner[routes[0, j]], jnp.int32).astype(F32)
    kept = lax.broadcasted_iota(jnp.int32, (block, width), 0) < ranks[0]

    @pl.when(row == 0)
    def _():
        at = lax.broadcasted_iota(jnp.int32, (piece_rows, width), 0) + piece * piece_rows
        unit = at == lax.broadcasted_iota(jnp.int32, (piece_rows, width), 1)
        chain_in[...] = jnp.where(unit, 1.0, 0.0).astype(BF16)

    pl.semaphore_wait(barrier, rows - 1 + sectors - 1)

    def chain_copy():
        return pltpu.make_async_remote_copy(
            src_ref=pairs.at[piece], dst_ref=chain_in, send_sem=chain_send, recv_sem=chain_recv,
            device_id=(lax.rem(row + 1, rows), sector), device_id_type=MESH)

    def left_copy(slot, target):
        return pltpu.make_async_remote_copy(
            src_ref=left_bf, dst_ref=left_in.at[slot], send_sem=left_send.at[target], recv_sem=left_recv.at[slot],
            device_id=(target, sector), device_id_type=MESH)

    def info_copy(slot, step, target):
        return pltpu.make_async_remote_copy(
            src_ref=info.at[slot], dst_ref=info.at[slot], send_sem=info_send.at[step], recv_sem=info_recv.at[slot],
            device_id=(row, target), device_id_type=MESH)

    def pair_copy(slot, step, target):
        return pltpu.make_async_remote_copy(
            src_ref=pairs.at[slot], dst_ref=pairs.at[slot], send_sem=pair_send.at[step], recv_sem=pair_recv.at[slot],
            device_id=(row, target), device_id_type=MESH)

    def y_copy(slot, sem, target):
        return pltpu.make_async_remote_copy(
            src_ref=ys.at[slot], dst_ref=ys.at[slot], send_sem=sem, recv_sem=y_recv.at[slot],
            device_id=(row, target), device_id_type=MESH)

    for target in range(rows - 1, 0, -1):
        @pl.when(row < target)
        def _():
            left_copy(row, target).start()
    for step in range(1, sectors):
        info_copy(sector, step, lax.rem(sector + step, sectors)).start()

    @pl.when(row > 0)
    def _():
        chain_copy().wait_recv()
    before = chain_in[...]
    product = 0.9 * before.astype(F32) + jnp.dot(before, right_bf[...], preferred_element_type=F32)
    pairs[piece] = product.astype(BF16)

    @pl.when(row < rows - 1)
    def _():
        chain_copy().start()
    for step in range(1, slices):
        pair_copy(piece, step, group_base + partner(piece, step, slices)[0]).start()

    y_f32[...] = jnp.where(kept, boundary_in[0], 0.0)

    def apply_left(factor):
        value = y_f32[...]
        moved = jnp.dot(factor, value.astype(BF16), preferred_element_type=F32)
        return jnp.where(kept, 0.9 * value + moved, 0.0)

    for source in range(rows - 1):
        @pl.when(source < row)
        def _():
            left_copy(source, source + 1).wait_recv()
            y_f32[...] = apply_left(left_in[source])
    ys[sector] = apply_left(left_bf[...]).astype(BF16)

    for step in range(groups - 1, 0, -1):
        y_copy(sector, y_send.at[step], partner(group, step, groups)[0] * 2 + core).start()
    y_copy(sector, y_send.at[0], twin).start()

    for step in range(1, sectors):
        source = lax.rem(sector + step, sectors)
        info_copy(source, step, source).wait_recv()
    me = sector.astype(F32)
    for source in range(sectors):
        picked = jnp.zeros((width, width), BF16)
        for j in range(slots):
            mark = info[source, pl.ds(j, 1), :]
            mark = jnp.concatenate([mark] * (width // 128), axis=1)
            same = jnp.where(mark == me, 1.0, 0.0).astype(BF16)
            picked = picked + weight[0, j] * same
        chosen[source] = picked

    for step in range(groups - 1, 0, -1):
        slot = partner(group, step, groups)[1] * 2 + core
        y_copy(slot, y_send.at[step], slot).wait_recv()
        y_copy(slot, twin_send.at[step], twin).start()

    for step in range(1, slices):
        slot = partner(piece, step, slices)[1]
        pair_copy(slot, step, group_base + slot).wait_recv()
    all_pairs = pairs[...].reshape(width, width)

    def term(slot, first=False):
        moved = jnp.dot(ys[slot], all_pairs, preferred_element_type=F32)
        if first:
            bound_out[0, 0] = moved
        return jnp.dot(moved.astype(BF16), chosen[slot], preferred_element_type=F32).astype(BF16).astype(F32)

    total = term(sector, True)
    for step in range(groups - 1, 0, -1):
        total = total + term(partner(group, step, groups)[1] * 2 + core)
    y_copy(twin, y_send.at[0], twin).wait_recv()
    total = total + term(twin)
    for step in range(groups - 1, 0, -1):
        slot = partner(group, step, groups)[1] * 2 + 1 - core
        y_copy(slot, twin_send.at[step], twin).wait_recv()
        total = total + term(slot)
    env_out[0, 0] = total

    for target in range(1, rows):
        @pl.when(row < target)
        def _():
            left_copy(row, target).wait_send()

    @pl.when(row < rows - 1)
    def _():
        chain_copy().wait_send()
    for step in range(1, sectors):
        info_copy(sector, step, lax.rem(sector + step, sectors)).wait_send()
    for step in range(1, slices):
        pair_copy(piece, step, group_base + partner(piece, step, slices)[0]).wait_send()
    y_copy(sector, y_send.at[0], twin).wait_send()
    for step in range(1, groups):
        y_copy(sector, y_send.at[step], partner(group, step, groups)[0] * 2 + core).wait_send()
        y_copy(partner(group, step, groups)[1] * 2 + core, twin_send.at[step], twin).wait_send()


def solution(mesh):
    rows, sectors = mesh.shape["row"], mesh.shape["sector"]

    def on_device(boundary_in, left, right, weight, ranks, routes, owner):
        block, width = boundary_in.shape[1:]
        slots = weight.shape[1]
        slices = min(sectors, width // 16)
        out = jax.ShapeDtypeStruct((1, 1, block, width), F32)
        vmem, smem = pl.BlockSpec(memory_space=pltpu.VMEM), pl.BlockSpec(memory_space=pltpu.SMEM)
        dma = pltpu.SemaphoreType.DMA
        return pl.pallas_call(
            functools.partial(kernel, rows, sectors, slices),
            out_shape=(out, out),
            in_specs=[smem] * 3 + [vmem] * 4,
            out_specs=(vmem, vmem),
            scratch_shapes=[
                pltpu.VMEM((block, block), BF16),
                pltpu.VMEM((rows - 1, block, block), BF16),
                pltpu.VMEM((width, width), BF16),
                pltpu.VMEM((block, width), F32),
                pltpu.VMEM((width // slices, width), BF16),
                pltpu.VMEM((slices, width // slices, width), BF16),
                pltpu.VMEM((sectors, block, width), BF16),
                pltpu.VMEM((sectors, max(8, slots), 128), F32),
                pltpu.VMEM((sectors, width, width), BF16),
                dma((rows,)), dma((rows,)), dma, dma, dma((slices,)), dma((slices,)),
                dma((sectors // 2,)), dma((sectors,)), dma((sectors // 2,)), dma((sectors,)), dma((sectors,)),
            ],
            compiler_params=pltpu.CompilerParams(
                collective_id=0, has_side_effects=True, vmem_limit_bytes=32 * 2**20),
        )(ranks, routes, owner, boundary_in, left, right, weight)

    return jax.shard_map(
        on_device,
        mesh=mesh,
        in_specs=(
            P("sector", None, None),
            P("row", "sector", None, None),
            P("row", None, None),
            P("row", None, None, None),
            P("sector"),
            P("sector", None),
            P(),
        ),
        out_specs=(P("row", "sector", None, None), P("row", "sector", None, None)),
        check_vma=False,
    )
```

time: 43.9 us -> 27.2 us (0.62)
  the two profiles are of different devices: /device:TPU:0 before, /device:TPU:25 now
where the time goes in v1:
time: 27.2 us; the launch traced here: 27 us
  Pallas kernels  20.6 us (76%)
  local copies, waits for them, and re-layouts  5.05 us (19%)
  between operations  1.35 us (5%)
    pallas_call x1, Pallas kernels, on_device(): pl.pallas_call(functools.partial(kernel, rows, sectors, slices), out_shap...  20.6 us
    unnamed x14, local copies, waits for them, and re-layouts  5.05 us

profile of v1, /device:TPU:25, one launch (start us, length us, event | category | flops | bytes accessed | tf_op | source)
XLA Modules:
  0.0 27.0 jit_solution(4032163740893497098)
XLA Ops:
  0.6 0.0 copy-start.5
  0.6 0.0 copy-start.4
  1.3 0.0 copy-done.5
  1.3 0.0 copy-done.4
  1.3 0.0 copy-start
  1.3 1.0 %copy-done = bf16[1,4,256,256]{3,2,1,0:T(8,128)(2,1)S(1)} copy-done((bf16[1,4,256,256]{3,2,1,0:T(8,128)(2,1)S(1)}, bf16[1,4,256,256]{3,2,1,0:T(8,128)(2,1)}, u32[]{:S(2)}) %copy-start) | copy-done | bytes 524312
  2.4 0.0 copy-start.1
  2.4 0.9 %copy-done.1 = f32[1,256,256]{2,1,0:T(8,128)S(1)} copy-done((f32[1,256,256]{2,1,0:T(8,128)S(1)}, f32[1,256,256]{2,1,0:T(8,128)}, u32[]{:S(2)}) %copy-start.1) | copy-done | bytes 262168
  3.3 0.0 copy-start.2
  3.3 0.9 %copy-done.2 = f32[1,128,256]{2,1,0:T(8,128)S(1)} copy-done((f32[1,128,256]{2,1,0:T(8,128)S(1)}, f32[1,128,256]{2,1,0:T(8,128)}, u32[]{:S(2)}) %copy-start.2) | copy-done | bytes 131096
  4.2 0.0 copy-start.3
  4.2 0.8 %copy-done.3 = f32[1,1,128,128]{3,2,1,0:T(8,128)S(1)} copy-done((f32[1,1,128,128]{3,2,1,0:T(8,128)S(1)}, f32[1,1,128,128]{3,2,1,0:T(8,128)}, u32[]{:S(2)}) %copy-start.3) | copy-done | bytes 65560
  5.1 20.6 %shard_map.86 = (f32[1,1,128,256]{3,2,1,0:T(8,128)S(1)}, f32[1,1,128,256]{3,2,1,0:T(8,128)S(1)}) custom-call(s32[1]{0:T(128)S(6)} %copy.11.ranks, s32[1,4]{1,0:T(1,128)S(1)} %copy-done.4, s32[8]{0:T(128)S(1)} %copy-done.5, f32[1,128,256]{2,1,0:T(8,128)S(1)} %copy-done.2, f32[1,1,128,128]{3,2,1,0:T(8,128)S(1)} %copy-done.3, f32[1,256,256]{2,1,0:T(8,128)S(1)} %copy-done.1, ...), custom_call_target="tpu_custom_call" | custom-call | tf_op jit(solution)/shard_map/pallas_call | solution.py:195
  25.7 0.7 %copy.12 = f32[1,1,128,256]{3,2,1,0:T(8,128)} copy(f32[1,1,128,256]{3,2,1,0:T(8,128)S(1)} %get-tuple-element.4) | data formatting | bytes 262144
  26.3 0.7 %copy.13 = f32[1,1,128,256]{3,2,1,0:T(8,128)} copy(f32[1,1,128,256]{3,2,1,0:T(8,128)S(1)} %get-tuple-element.5) | data formatting | bytes 262144
Async XLA Ops:
  0.6 0.7 %copy-start.5 = (s32[8]{0:T(128)S(1)}, s32[8]{0:T(128)}, u32[]{:S(2)}) copy-start(s32[8]{0:T(128)} %owner.1) | copy-start | bytes 100
  0.6 0.7 %copy-start.4 = (s32[1,4]{1,0:T(1,128)S(1)}, s32[1,4]{1,0:T(1,128)}, u32[]{:S(2)}) copy-start(s32[1,4]{1,0:T(1,128)} %routes.1) | copy-start | bytes 52
  1.3 1.0 %copy-start = (bf16[1,4,256,256]{3,2,1,0:T(8,128)(2,1)S(1)}, bf16[1,4,256,256]{3,2,1,0:T(8,128)(2,1)}, u32[]{:S(2)}) copy-start(bf16[1,4,256,256]{3,2,1,0:T(8,128)(2,1)} %weight.1) | copy-start | bytes 1572868
  2.4 0.9 %copy-start.1 = (f32[1,256,256]{2,1,0:T(8,128)S(1)}, f32[1,256,256]{2,1,0:T(8,128)}, u32[]{:S(2)}) copy-start(f32[1,256,256]{2,1,0:T(8,128)} %right.1) | copy-start | bytes 786436
  3.3 0.9 %copy-start.2 = (f32[1,128,256]{2,1,0:T(8,128)S(1)}, f32[1,128,256]{2,1,0:T(8,128)}, u32[]{:S(2)}) copy-start(f32[1,128,256]{2,1,0:T(8,128)} %boundary_in.1) | copy-start | bytes 393220
  4.2 0.8 %copy-start.3 = (f32[1,1,128,128]{3,2,1,0:T(8,128)S(1)}, f32[1,1,128,128]{3,2,1,0:T(8,128)}, u32[]{:S(2)}) copy-start(f32[1,1,128,128]{3,2,1,0:T(8,128)} %left.1) | copy-start | bytes 196612

commit v2 on v1

v2 whole, which is shorter than its diff:
```python
import functools

import jax
import jax.numpy as jnp
from jax import lax
from jax.experimental import pallas as pl
from jax.experimental.pallas import tpu as pltpu
from jax.sharding import PartitionSpec as P

MESH = pl.DeviceIdType.MESH
BF16 = jnp.bfloat16
F32 = jnp.float32


def partner(index, step, count):
    if count & (count - 1):
        return lax.rem(index + step, count), lax.rem(index - step + count, count)
    result, bit = 0, 1
    while bit < count:
        own = lax.rem(index // bit, 2)
        result = result + ((1 - own) if step & bit else own) * bit
        bit *= 2
    return result, result


def kernel(
    rows, sectors, slices,
    ranks_hbm, routes_hbm, owner_hbm, boundary_hbm, left_hbm, right_hbm, weight_hbm,
    bound_out, env_out,
    ranks, routes, owner, boundary, left, right, weight, in_sem,
    left_bf, left_in, right_bf, product, chain_in, pairs, starts, prefixes, moved, info, chosen,
    left_send, left_recv, chain_send, chain_recv, pair_send, pair_recv,
    start_send, start_recv, start_twin, prefix_send, prefix_recv, prefix_twin, info_send, info_recv,
):
    row, sector = lax.axis_index("row"), lax.axis_index("sector")
    slots = weight.shape[1]
    block, width = boundary.shape[1], boundary.shape[2]
    piece_rows = width // slices
    piece = lax.rem(sector, slices)
    group_base = sector - piece
    groups = sectors // 2
    group, core = sector // 2, lax.rem(sector, 2)
    twin = group * 2 + 1 - core

    barrier = pltpu.get_barrier_semaphore()
    for step in range(1, rows):
        pl.semaphore_signal(barrier, inc=1, device_id=(lax.rem(row + step, rows), sector), device_id_type=MESH)
    for step in range(1, sectors):
        pl.semaphore_signal(barrier, inc=1, device_id=(row, lax.rem(sector + step, sectors)), device_id_type=MESH)

    loads = [
        pltpu.make_async_copy(source, target, in_sem.at[at])
        for at, (source, target) in enumerate((
            (right_hbm, right), (left_hbm, left), (boundary_hbm, boundary), (ranks_hbm, ranks),
            (routes_hbm, routes), (owner_hbm, owner), (weight_hbm, weight)))
    ]
    for load in loads:
        load.start()
    loads[0].wait()
    right_bf[...] = right[0].astype(BF16)
    loads[1].wait()
    left_bf[...] = left[0, 0].astype(BF16)
    loads[2].wait()
    starts[sector] = boundary[0].astype(BF16)
    for load in loads[3:6]:
        load.wait()
    for j in range(slots):
        info[sector, pl.ds(j, 1), :] = jnp.full((1, 128), owner[routes[0, j]], jnp.int32).astype(F32)

    @pl.when(row == 0)
    def _():
        at = lax.broadcasted_iota(jnp.int32, (piece_rows, width), 0) + piece * piece_rows
        unit = at == lax.broadcasted_iota(jnp.int32, (piece_rows, width), 1)
        chain_in[...] = jnp.where(unit, 1.0, 0.0).astype(BF16)

    pl.semaphore_wait(barrier, rows - 1 + sectors - 1)

    def chain_copy():
        return pltpu.make_async_remote_copy(
            src_ref=pairs.at[piece], dst_ref=chain_in, send_sem=chain_send, recv_sem=chain_recv,
            device_id=(lax.rem(row + 1, rows), sector), device_id_type=MESH)

    def left_copy(slot, target):
        return pltpu.make_async_remote_copy(
            src_ref=left_bf, dst_ref=left_in.at[slot], send_sem=left_send.at[target], recv_sem=left_recv.at[slot],
            device_id=(target, sector), device_id_type=MESH)

    def in_plane(buffer, slot, send_sem, recv_sem, target):
        return pltpu.make_async_remote_copy(
            src_ref=buffer.at[slot], dst_ref=buffer.at[slot], send_sem=send_sem, recv_sem=recv_sem.at[slot],
            device_id=(row, target), device_id_type=MESH)

    def info_copy(slot, step, target):
        return in_plane(info, slot, info_send.at[step], info_recv, target)

    def pair_copy(slot, step, target):
        return in_plane(pairs, slot, pair_send.at[step], pair_recv, target)

    def start_copy(slot, sem, target):
        return in_plane(starts, slot, sem, start_recv, target)

    def prefix_copy(slot, sem, target):
        return in_plane(prefixes, slot, sem, prefix_recv, target)

    def chain_step():
        @pl.when(row > 0)
        def _():
            chain_copy().wait_recv()
        before = chain_in[...]
        after = 0.9 * before.astype(F32) + jnp.dot(before, right_bf[...], preferred_element_type=F32)
        pairs[piece] = after.astype(BF16)

        @pl.when(row < rows - 1)
        def _():
            chain_copy().start()
        for step in range(1, slices):
            pair_copy(piece, step, group_base + partner(piece, step, slices)[0]).start()

    pl.when(row == 0)(chain_step)

    for target in range(rows - 1, 0, -1):
        @pl.when(row < target)
        def _():
            left_copy(row, target).start()
    for step in range(groups - 1, 0, -1):
        start_copy(sector, start_send.at[step], partner(group, step, groups)[0] * 2 + core).start()
    start_copy(sector, start_send.at[0], twin).start()
    for step in range(1, sectors):
        info_copy(sector, step, lax.rem(sector + step, sectors)).start()

    pl.when((row > 0) & (row < rows - 1))(chain_step)

    across = lax.broadcasted_iota(jnp.int32, (block, block), 1)
    down = lax.broadcasted_iota(jnp.int32, (block, block), 0)
    kept = across < ranks[0]
    own = jnp.where(across == down, 0.9, 0.0) + left[0, 0]
    product[...] = jnp.where(kept & (down < ranks[0]), own, 0.0)
    for source in range(rows - 2, -1, -1):
        @pl.when(source < row)
        def _():
            left_copy(source, source + 1).wait_recv()
            value = product[...]
            change = jnp.dot(value.astype(BF16), left_in[source], preferred_element_type=F32)
            product[...] = jnp.where(kept, 0.9 * value + change, 0.0)
    prefixes[sector] = product[...].astype(BF16)
    for step in range(groups - 1, 0, -1):
        prefix_copy(sector, prefix_send.at[step], partner(group, step, groups)[0] * 2 + core).start()
    prefix_copy(sector, prefix_send.at[0], twin).start()

    pl.when((row > 0) & (row == rows - 1))(chain_step)

    for step in range(groups - 1, 0, -1):
        slot = partner(group, step, groups)[1] * 2 + core
        start_copy(slot, start_send.at[step], slot).wait_recv()
        start_copy(slot, start_twin.at[step], twin).start()

    loads[6].wait()
    for step in range(1, sectors):
        source = lax.rem(sector + step, sectors)
        info_copy(source, step, source).wait_recv()
    me = sector.astype(F32)
    for source in range(sectors):
        picked = jnp.zeros((width, width), BF16)
        for j in range(slots):
            mark = info[source, pl.ds(j, 1), :]
            mark = jnp.concatenate([mark] * (width // 128), axis=1)
            same = jnp.where(mark == me, 1.0, 0.0).astype(BF16)
            picked = picked + weight[0, j] * same
        chosen[source] = picked

    for step in range(groups - 1, 0, -1):
        slot = partner(group, step, groups)[1] * 2 + core
        prefix_copy(slot, prefix_send.at[step], slot).wait_recv()
        prefix_copy(slot, prefix_twin.at[step], twin).start()

    start_copy(twin, start_send.at[0], twin).wait_recv()
    for step in range(groups - 1, 0, -1):
        start_copy(partner(group, step, groups)[1] * 2 + 1 - core, start_twin.at[step], twin).wait_recv()
    for step in range(1, slices):
        slot = partner(piece, step, slices)[1]
        pair_copy(slot, step, group_base + slot).wait_recv()
    all_pairs = pairs[...].reshape(width, width)
    for source in range(sectors):
        moved[source] = jnp.dot(starts[source], all_pairs, preferred_element_type=F32).astype(BF16)

    def term(slot, first=False):
        value = jnp.dot(prefixes[slot], moved[slot], preferred_element_type=F32)
        if first:
            bound_out[0, 0] = value
        return jnp.dot(value.astype(BF16), chosen[slot], preferred_element_type=F32).astype(BF16).astype(F32)

    total = term(sector, True)
    for step in range(groups - 1, 0, -1):
        total = total + term(partner(group, step, groups)[1] * 2 + core)
    prefix_copy(twin, prefix_send.at[0], twin).wait_recv()
    total = total + term(twin)
    for step in range(groups - 1, 0, -1):
        slot = partner(group, step, groups)[1] * 2 + 1 - core
        prefix_copy(slot, prefix_twin.at[step], twin).wait_recv()
        total = total + term(slot)
    env_out[0, 0] = total

    for target in range(1, rows):
        @pl.when(row < target)
        def _():
            left_copy(row, target).wait_send()

    @pl.when(row < rows - 1)
    def _():
        chain_copy().wait_send()
    for step in range(1, sectors):
        info_copy(sector, step, lax.rem(sector + step, sectors)).wait_send()
    for step in range(1, slices):
        pair_copy(piece, step, group_base + partner(piece, step, slices)[0]).wait_send()
    for copy, first, second in ((start_copy, start_send, start_twin), (prefix_copy, prefix_send, prefix_twin)):
        copy(sector, first.at[0], twin).wait_send()
        for step in range(1, groups):
            to, source = partner(group, step, groups)
            copy(sector, first.at[step], to * 2 + core).wait_send()
            copy(source * 2 + core, second.at[step], twin).wait_send()


def solution(mesh):
    rows, sectors = mesh.shape["row"], mesh.shape["sector"]

    def on_device(boundary_in, left, right, weight, ranks, routes, owner):
        block, width = boundary_in.shape[1:]
        slots = weight.shape[1]
        slices = min(sectors, width // 16)
        out = jax.ShapeDtypeStruct((1, 1, block, width), F32)
        vmem = pl.BlockSpec(memory_space=pltpu.VMEM)
        dma = pltpu.SemaphoreType.DMA
        operands = (ranks, routes, owner, boundary_in, left, right, weight)
        return pl.pallas_call(
            functools.partial(kernel, rows, sectors, slices),
            out_shape=(out, out),
            in_specs=[pl.BlockSpec(memory_space=pltpu.HBM)] * len(operands),
            out_specs=(vmem, vmem),
            scratch_shapes=[
                *(pltpu.SMEM(operand.shape, operand.dtype) for operand in operands[:3]),
                *(pltpu.VMEM(operand.shape, operand.dtype) for operand in operands[3:]),
                dma((len(operands),)),
                pltpu.VMEM((block, block), BF16),
                pltpu.VMEM((rows - 1, block, block), BF16),
                pltpu.VMEM((width, width), BF16),
                pltpu.VMEM((block, block), F32),
                pltpu.VMEM((width // slices, width), BF16),
                pltpu.VMEM((slices, width // slices, width), BF16),
                pltpu.VMEM((sectors, block, width), BF16),
                pltpu.VMEM((sectors, block, block), BF16),
                pltpu.VMEM((sectors, block, width), BF16),
                pltpu.VMEM((sectors, max(8, slots), 128), F32),
                pltpu.VMEM((sectors, width, width), BF16),
                dma((rows,)), dma((rows,)), dma, dma, dma((slices,)), dma((slices,)),
                dma((sectors // 2,)), dma((sectors,)), dma((sectors // 2,)),
                dma((sectors // 2,)), dma((sectors,)), dma((sectors // 2,)),
                dma((sectors,)), dma((sectors,)),
            ],
            compiler_params=pltpu.CompilerParams(
                collective_id=0, has_side_effects=True, vmem_limit_bytes=60 * 2**20),
        )(*operands)

    return jax.shard_map(
        on_device,
        mesh=mesh,
        in_specs=(
            P("sector", None, None),
            P("row", "sector", None, None),
            P("row", None, None),
            P("row", None, None, None),
            P("sector"),
            P("sector", None),
            P(),
        ),
        out_specs=(P("row", "sector", None, None), P("row", "sector", None, None)),
        check_vma=False,
    )
```

time: 27.2 us -> 22.6 us (0.83)
  local copies, waits for them, and re-layouts: 5.05 us -> 2.26 us
  Pallas kernels: 20.6 us -> 18.9 us
    unnamed x14 -> x4, local copies, waits for them, and re-layouts: 5.05 us -> 2.26 us
    pallas_call x1, Pallas kernels: 20.6 us -> 18.9 us  [on_device(): pl.pallas_call(functools.partial(kernel, rows, sectors, slices), out_shap...]
where the time goes in v2:
time: 22.6 us; the launch traced here: 22.5 us
  Pallas kernels  18.9 us (84%)
  local copies, waits for them, and re-layouts  2.26 us (10%)
  between operations  1.29 us (6%)
    pallas_call x1, Pallas kernels, on_device(): pl.pallas_call(functools.partial(kernel, rows, sectors, slices), out_shap...  18.9 us
    unnamed x4, local copies, waits for them, and re-layouts  2.26 us

profile of v2, /device:TPU:25, one launch (start us, length us, event | category | flops | bytes accessed | tf_op | source)
XLA Modules:
  0.0 22.5 jit_solution(8432362819585668090)
XLA Ops:
  1.3 18.9 %shard_map.86 = (f32[1,1,128,256]{3,2,1,0:T(8,128)}, f32[1,1,128,256]{3,2,1,0:T(8,128)}) custom-call(s32[1]{0:T(128)S(6)} %copy.11.ranks_hbm, s32[1,4]{1,0:T(1,128)} %routes_hbm.1, s32[8]{0:T(128)} %owner_hbm.1, f32[1,128,256]{2,1,0:T(8,128)} %boundary_hbm.1, f32[1,1,128,128]{3,2,1,0:T(8,128)} %left_hbm.1, f32[1,256,256]{2,1,0:T(8,128)} %right_hbm.1, ...), custom_call_target="tpu_custom_call" | custom-call | tf_op jit(solution)/shard_map/pallas_call | solution.py:234
  20.2 0.0 copy-start
  20.2 1.6 %copy.12 = f32[1,1,128,256]{3,2,1,0:T(8,128)} copy(f32[1,1,128,256]{3,2,1,0:T(8,128)} %get-tuple-element.4) | data formatting | bytes 262144
  21.8 0.0 copy-done
  21.8 0.7 %copy.13 = f32[1,1,128,256]{3,2,1,0:T(8,128)} copy(f32[1,1,128,256]{3,2,1,0:T(8,128)S(1)} %copy-done) | data formatting | bytes 262144
Async XLA Ops:
  20.2 1.6 %copy-start = (f32[1,1,128,256]{3,2,1,0:T(8,128)S(1)}, f32[1,1,128,256]{3,2,1,0:T(8,128)}, u32[]{:S(2)}) copy-start(f32[1,1,128,256]{3,2,1,0:T(8,128)} %get-tuple-element.5) | copy-start | bytes 393220

commit v3 on v2

--- a/solution.py
+++ b/solution.py
@@ -28,7 +28,7 @@
     ranks_hbm, routes_hbm, owner_hbm, boundary_hbm, left_hbm, right_hbm, weight_hbm,
     bound_out, env_out,
     ranks, routes, owner, boundary, left, right, weight, in_sem,
-    left_bf, left_in, right_bf, product, chain_in, pairs, starts, prefixes, moved, info, chosen,
+    left_bf, left_in, right_bf, product, chain_in, pairs, starts, prefixes, moved, terms, info, chosen,
     left_send, left_recv, chain_send, chain_recv, pair_send, pair_recv,
     start_send, start_recv, start_twin, prefix_send, prefix_recv, prefix_twin, info_send, info_recv,
 ):
@@ -130,30 +130,6 @@
 
     pl.when((row > 0) & (row < rows - 1))(chain_step)
 
-    across = lax.broadcasted_iota(jnp.int32, (block, block), 1)
-    down = lax.broadcasted_iota(jnp.int32, (block, block), 0)
-    kept = across < ranks[0]
-    own = jnp.where(across == down, 0.9, 0.0) + left[0, 0]
-    product[...] = jnp.where(kept & (down < ranks[0]), own, 0.0)
-    for source in range(rows - 2, -1, -1):
-        @pl.when(source < row)
-        def _():
-            left_copy(source, source + 1).wait_recv()
-            value = product[...]
-            change = jnp.dot(value.astype(BF16), left_in[source], preferred_element_type=F32)
-            product[...] = jnp.where(kept, 0.9 * value + change, 0.0)
-    prefixes[sector] = product[...].astype(BF16)
-    for step in range(groups - 1, 0, -1):
-        prefix_copy(sector, prefix_send.at[step], partner(group, step, groups)[0] * 2 + core).start()
-    prefix_copy(sector, prefix_send.at[0], twin).start()
-
-    pl.when((row > 0) & (row == rows - 1))(chain_step)
-
-    for step in range(groups - 1, 0, -1):
-        slot = partner(group, step, groups)[1] * 2 + core
-        start_copy(slot, start_send.at[step], slot).wait_recv()
-        start_copy(slot, start_twin.at[step], twin).start()
-
     loads[6].wait()
     for step in range(1, sectors):
         source = lax.rem(sector + step, sectors)
@@ -168,6 +144,30 @@
             picked = picked + weight[0, j] * same
         chosen[source] = picked
 
+    across = lax.broadcasted_iota(jnp.int32, (block, block), 1)
+    down = lax.broadcasted_iota(jnp.int32, (block, block), 0)
+    kept = across < ranks[0]
+    own = jnp.where(across == down, 0.9, 0.0) + left[0, 0]
+    product[...] = jnp.where(kept & (down < ranks[0]), own, 0.0)
+    for source in range(rows - 2, -1, -1):
+        @pl.when(source < row)
+        def _():
+            left_copy(source, source + 1).wait_recv()
+            value = product[...]
+            change = jnp.dot(value.astype(BF16), left_in[source], preferred_element_type=F32)
+            product[...] = jnp.where(kept, 0.9 * value + change, 0.0)
+    prefixes[sector] = product[...].astype(BF16)
+    for step in range(groups - 1, 0, -1):
+        prefix_copy(sector, prefix_send.at[step], partner(group, step, groups)[0] * 2 + core).start()
+    prefix_copy(sector, prefix_send.at[0], twin).start()
+
+    pl.when((row > 0) & (row == rows - 1))(chain_step)
+
+    for step in range(groups - 1, 0, -1):
+        slot = partner(group, step, groups)[1] * 2 + core
+        start_copy(slot, start_send.at[step], slot).wait_recv()
+        start_copy(slot, start_twin.at[step], twin).start()
+
     for step in range(groups - 1, 0, -1):
         slot = partner(group, step, groups)[1] * 2 + core
         prefix_copy(slot, prefix_send.at[step], slot).wait_recv()
@@ -181,23 +181,19 @@
         pair_copy(slot, step, group_base + slot).wait_recv()
     all_pairs = pairs[...].reshape(width, width)
     for source in range(sectors):
-        moved[source] = jnp.dot(starts[source], all_pairs, preferred_element_type=F32).astype(BF16)
-
-    def term(slot, first=False):
-        value = jnp.dot(prefixes[slot], moved[slot], preferred_element_type=F32)
-        if first:
-            bound_out[0, 0] = value
-        return jnp.dot(value.astype(BF16), chosen[slot], preferred_element_type=F32).astype(BF16).astype(F32)
-
-    total = term(sector, True)
-    for step in range(groups - 1, 0, -1):
-        total = total + term(partner(group, step, groups)[1] * 2 + core)
+        value = jnp.dot(starts[source], all_pairs, preferred_element_type=F32).astype(BF16)
+        moved[source] = value
+        terms[source] = jnp.dot(value, chosen[source], preferred_element_type=F32).astype(BF16)
+    bound_out[0, 0] = jnp.dot(prefixes[sector], moved[sector], preferred_element_type=F32)
+
     prefix_copy(twin, prefix_send.at[0], twin).wait_recv()
-    total = total + term(twin)
-    for step in range(groups - 1, 0, -1):
-        slot = partner(group, step, groups)[1] * 2 + 1 - core
-        prefix_copy(slot, prefix_twin.at[step], twin).wait_recv()
-        total = total + term(slot)
+    for step in range(groups - 1, 0, -1):
+        prefix_copy(partner(group, step, groups)[1] * 2 + 1 - core, prefix_twin.at[step], twin).wait_recv()
+    total = jnp.zeros((block, width), F32)
+    for first in range(0, sectors, 2):
+        both = jnp.concatenate([prefixes[first], prefixes[first + 1]], axis=1)
+        total = total + jnp.dot(
+            both, terms[pl.ds(first, 2)].reshape(2 * block, width), preferred_element_type=F32)
     env_out[0, 0] = total
 
     for target in range(1, rows):
@@ -227,7 +223,7 @@
         block, width = boundary_in.shape[1:]
         slots = weight.shape[1]
         slices = min(sectors, width // 16)
-        out = jax.ShapeDtypeStruct((1, 1, block, width), F32)
+        out = pltpu.VMEM((1, 1, block, width), F32)
         vmem = pl.BlockSpec(memory_space=pltpu.VMEM)
         dma = pltpu.SemaphoreType.DMA
         operands = (ranks, routes, owner, boundary_in, left, right, weight)
@@ -249,6 +245,7 @@
                 pltpu.VMEM((sectors, block, width), BF16),
                 pltpu.VMEM((sectors, block, block), BF16),
                 pltpu.VMEM((sectors, block, width), BF16),
+                pltpu.VMEM((sectors, block, width), BF16),
                 pltpu.VMEM((sectors, max(8, slots), 128), F32),
                 pltpu.VMEM((sectors, width, width), BF16),
                 dma((rows,)), dma((rows,)), dma, dma, dma((slices,)), dma((slices,)),

time: 22.6 us -> 20.4 us (0.903)
  the two profiles are of different devices: /device:TPU:25 before, /device:TPU:1 now
where the time goes in v3:
time: 20.4 us; the launch traced here: 20.2 us
  Pallas kernels  17.6 us (86%)
  local copies, waits for them, and re-layouts  1.31 us (6%)
  between operations  1.29 us (6%)
    pallas_call x1, Pallas kernels, on_device(): pl.pallas_call(functools.partial(kernel, rows, sectors, slices), out_shap...  17.6 us
    unnamed x2, local copies, waits for them, and re-layouts  1.31 us

profile of v3, /device:TPU:1, one launch (start us, length us, event | category | flops | bytes accessed | tf_op | source)
XLA Modules:
  0.0 20.2 jit_solution(9109771169971353594)
XLA Ops:
  1.3 17.6 %shard_map.86 = (f32[1,1,128,256]{3,2,1,0:T(8,128)S(1)}, f32[1,1,128,256]{3,2,1,0:T(8,128)S(1)}) custom-call(s32[1]{0:T(128)S(6)} %copy.13.ranks_hbm, s32[1,4]{1,0:T(1,128)} %routes_hbm.1, s32[8]{0:T(128)} %owner_hbm.1, f32[1,128,256]{2,1,0:T(8,128)} %boundary_hbm.1, f32[1,1,128,128]{3,2,1,0:T(8,128)} %left_hbm.1, f32[1,256,256]{2,1,0:T(8,128)} %right_hbm.1, ...), custom_call_target="tpu_custom_call" | custom-call | tf_op jit(solution)/shard_map/pallas_call | solution.py:230
  18.9 0.7 %copy.11 = f32[1,1,128,256]{3,2,1,0:T(8,128)} copy(f32[1,1,128,256]{3,2,1,0:T(8,128)S(1)} %get-tuple-element.2) | data formatting | bytes 262144
  19.6 0.7 %copy.12 = f32[1,1,128,256]{3,2,1,0:T(8,128)} copy(f32[1,1,128,256]{3,2,1,0:T(8,128)S(1)} %get-tuple-element.3) | data formatting | bytes 262144

commit v4 on v3

--- a/solution.py
+++ b/solution.py
@@ -69,6 +69,11 @@
 
     @pl.when(row == 0)
     def _():
+        masked = jnp.where(lax.broadcasted_iota(jnp.int32, (block, width), 0) < ranks[0], boundary[0], 0.0)
+        change = jnp.dot(left_bf[...], masked.astype(BF16), preferred_element_type=F32)
+        full = jnp.where(
+            lax.broadcasted_iota(jnp.int32, (block, width), 0) < ranks[0], 0.9 * masked + change, 0.0)
+        starts[sector] = full.astype(BF16)
         at = lax.broadcasted_iota(jnp.int32, (piece_rows, width), 0) + piece * piece_rows
         unit = at == lax.broadcasted_iota(jnp.int32, (piece_rows, width), 1)
         chain_in[...] = jnp.where(unit, 1.0, 0.0).astype(BF16)
@@ -118,10 +123,6 @@
 
     pl.when(row == 0)(chain_step)
 
-    for target in range(rows - 1, 0, -1):
-        @pl.when(row < target)
-        def _():
-            left_copy(row, target).start()
     for step in range(groups - 1, 0, -1):
         start_copy(sector, start_send.at[step], partner(group, step, groups)[0] * 2 + core).start()
     start_copy(sector, start_send.at[0], twin).start()
@@ -130,6 +131,10 @@
 
     pl.when((row > 0) & (row < rows - 1))(chain_step)
 
+    for target in range(rows - 1, 0, -1):
+        @pl.when(row < target)
+        def _():
+            left_copy(row, target).start()
     loads[6].wait()
     for step in range(1, sectors):
         source = lax.rem(sector + step, sectors)
@@ -157,9 +162,12 @@
             change = jnp.dot(value.astype(BF16), left_in[source], preferred_element_type=F32)
             product[...] = jnp.where(kept, 0.9 * value + change, 0.0)
     prefixes[sector] = product[...].astype(BF16)
-    for step in range(groups - 1, 0, -1):
-        prefix_copy(sector, prefix_send.at[step], partner(group, step, groups)[0] * 2 + core).start()
-    prefix_copy(sector, prefix_send.at[0], twin).start()
+
+    @pl.when(row > 0)
+    def _():
+        for step in range(groups - 1, 0, -1):
+            prefix_copy(sector, prefix_send.at[step], partner(group, step, groups)[0] * 2 + core).start()
+        prefix_copy(sector, prefix_send.at[0], twin).start()
 
     pl.when((row > 0) & (row == rows - 1))(chain_step)
 
@@ -168,10 +176,12 @@
         start_copy(slot, start_send.at[step], slot).wait_recv()
         start_copy(slot, start_twin.at[step], twin).start()
 
-    for step in range(groups - 1, 0, -1):
-        slot = partner(group, step, groups)[1] * 2 + core
-        prefix_copy(slot, prefix_send.at[step], slot).wait_recv()
-        prefix_copy(slot, prefix_twin.at[step], twin).start()
+    @pl.when(row > 0)
+    def _():
+        for step in range(groups - 1, 0, -1):
+            slot = partner(group, step, groups)[1] * 2 + core
+            prefix_copy(slot, prefix_send.at[step], slot).wait_recv()
+            prefix_copy(slot, prefix_twin.at[step], twin).start()
 
     start_copy(twin, start_send.at[0], twin).wait_recv()
     for step in range(groups - 1, 0, -1):
@@ -184,17 +194,27 @@
         value = jnp.dot(starts[source], all_pairs, preferred_element_type=F32).astype(BF16)
         moved[source] = value
         terms[source] = jnp.dot(value, chosen[source], preferred_element_type=F32).astype(BF16)
-    bound_out[0, 0] = jnp.dot(prefixes[sector], moved[sector], preferred_element_type=F32)
-
-    prefix_copy(twin, prefix_send.at[0], twin).wait_recv()
-    for step in range(groups - 1, 0, -1):
-        prefix_copy(partner(group, step, groups)[1] * 2 + 1 - core, prefix_twin.at[step], twin).wait_recv()
-    total = jnp.zeros((block, width), F32)
-    for first in range(0, sectors, 2):
-        both = jnp.concatenate([prefixes[first], prefixes[first + 1]], axis=1)
-        total = total + jnp.dot(
-            both, terms[pl.ds(first, 2)].reshape(2 * block, width), preferred_element_type=F32)
-    env_out[0, 0] = total
+
+    @pl.when(row == 0)
+    def _():
+        bound_out[0, 0] = jnp.dot(starts[sector], all_pairs, preferred_element_type=F32)
+        total = terms[0].astype(F32)
+        for source in range(1, sectors):
+            total = total + terms[source].astype(F32)
+        env_out[0, 0] = total
+
+    @pl.when(row > 0)
+    def _():
+        bound_out[0, 0] = jnp.dot(prefixes[sector], moved[sector], preferred_element_type=F32)
+        prefix_copy(twin, prefix_send.at[0], twin).wait_recv()
+        for step in range(groups - 1, 0, -1):
+            prefix_copy(partner(group, step, groups)[1] * 2 + 1 - core, prefix_twin.at[step], twin).wait_recv()
+        total = jnp.zeros((block, width), F32)
+        for first in range(0, sectors, 2):
+            both = jnp.concatenate([prefixes[first], prefixes[first + 1]], axis=1)
+            total = total + jnp.dot(
+                both, terms[pl.ds(first, 2)].reshape(2 * block, width), preferred_element_type=F32)
+        env_out[0, 0] = total
 
     for target in range(1, rows):
         @pl.when(row < target)
@@ -208,12 +228,16 @@
         info_copy(sector, step, lax.rem(sector + step, sectors)).wait_send()
     for step in range(1, slices):
         pair_copy(piece, step, group_base + partner(piece, step, slices)[0]).wait_send()
-    for copy, first, second in ((start_copy, start_send, start_twin), (prefix_copy, prefix_send, prefix_twin)):
+
+    def all_left(copy, first, second):
         copy(sector, first.at[0], twin).wait_send()
         for step in range(1, groups):
             to, source = partner(group, step, groups)
             copy(sector, first.at[step], to * 2 + core).wait_send()
             copy(source * 2 + core, second.at[step], twin).wait_send()
+
+    all_left(start_copy, start_send, start_twin)
+    pl.when(row > 0)(functools.partial(all_left, prefix_copy, prefix_send, prefix_twin))
 
 
 def solution(mesh):

time: 20.4 us -> 21.4 us (1.049)
  the two profiles are of different devices: /device:TPU:1 before, /device:TPU:25 now
where the time goes in v4:
time: 21.4 us; the launch traced here: 21.3 us
  Pallas kernels  18.7 us (87%)
  local copies, waits for them, and re-layouts  1.31 us (6%)
  between operations  1.29 us (6%)
    pallas_call x1, Pallas kernels, on_device(): pl.pallas_call(functools.partial(kernel, rows, sectors, slices), out_shap...  18.7 us
    unnamed x2, local copies, waits for them, and re-layouts  1.31 us

profile of v4, /device:TPU:25, one launch (start us, length us, event | category | flops | bytes accessed | tf_op | source)
XLA Modules:
  0.0 21.3 jit_solution(18133862242817584133)
XLA Ops:
  1.3 18.7 %shard_map.86 = (f32[1,1,128,256]{3,2,1,0:T(8,128)S(1)}, f32[1,1,128,256]{3,2,1,0:T(8,128)S(1)}) custom-call(s32[1]{0:T(128)S(6)} %copy.13.ranks_hbm, s32[1,4]{1,0:T(1,128)} %routes_hbm.1, s32[8]{0:T(128)} %owner_hbm.1, f32[1,128,256]{2,1,0:T(8,128)} %boundary_hbm.1, f32[1,1,128,128]{3,2,1,0:T(8,128)} %left_hbm.1, f32[1,256,256]{2,1,0:T(8,128)} %right_hbm.1, ...), custom_call_target="tpu_custom_call" | custom-call | tf_op jit(solution)/shard_map/pallas_call | solution.py:254
  19.9 0.7 %copy.11 = f32[1,1,128,256]{3,2,1,0:T(8,128)} copy(f32[1,1,128,256]{3,2,1,0:T(8,128)S(1)} %get-tuple-element.2) | data formatting | bytes 262144
  20.6 0.7 %copy.12 = f32[1,1,128,256]{3,2,1,0:T(8,128)} copy(f32[1,1,128,256]{3,2,1,0:T(8,128)S(1)} %get-tuple-element.3) | data formatting | bytes 262144

commit v5 on v4

--- a/solution.py
+++ b/solution.py
@@ -123,18 +123,18 @@
 
     pl.when(row == 0)(chain_step)
 
+    for target in range(rows - 1, 0, -1):
+        @pl.when(row < target)
+        def _():
+            left_copy(row, target).start()
     for step in range(groups - 1, 0, -1):
         start_copy(sector, start_send.at[step], partner(group, step, groups)[0] * 2 + core).start()
     start_copy(sector, start_send.at[0], twin).start()
     for step in range(1, sectors):
         info_copy(sector, step, lax.rem(sector + step, sectors)).start()
 
-    pl.when((row > 0) & (row < rows - 1))(chain_step)
-
-    for target in range(rows - 1, 0, -1):
-        @pl.when(row < target)
-        def _():
-            left_copy(row, target).start()
+    pl.when(row > 0)(chain_step)
+
     loads[6].wait()
     for step in range(1, sectors):
         source = lax.rem(sector + step, sectors)
@@ -169,8 +169,6 @@
             prefix_copy(sector, prefix_send.at[step], partner(group, step, groups)[0] * 2 + core).start()
         prefix_copy(sector, prefix_send.at[0], twin).start()
 
-    pl.when((row > 0) & (row == rows - 1))(chain_step)
-
     for step in range(groups - 1, 0, -1):
         slot = partner(group, step, groups)[1] * 2 + core
         start_copy(slot, start_send.at[step], slot).wait_recv()
@@ -240,6 +238,17 @@
     pl.when(row > 0)(functools.partial(all_left, prefix_copy, prefix_send, prefix_twin))
 
 
+def store(bound, env, bound_out, env_out, sem):
+    copies = [
+        pltpu.make_async_copy(bound, bound_out, sem.at[0]),
+        pltpu.make_async_copy(env, env_out, sem.at[1]),
+    ]
+    for copy in copies:
+        copy.start()
+    for copy in copies:
+        copy.wait()
+
+
 def solution(mesh):
     rows, sectors = mesh.shape["row"], mesh.shape["sector"]
 
@@ -251,7 +260,7 @@
         vmem = pl.BlockSpec(memory_space=pltpu.VMEM)
         dma = pltpu.SemaphoreType.DMA
         operands = (ranks, routes, owner, boundary_in, left, right, weight)
-        return pl.pallas_call(
+        results = pl.pallas_call(
             functools.partial(kernel, rows, sectors, slices),
             out_shape=(out, out),
             in_specs=[pl.BlockSpec(memory_space=pltpu.HBM)] * len(operands),
@@ -280,6 +289,14 @@
             compiler_params=pltpu.CompilerParams(
                 collective_id=0, has_side_effects=True, vmem_limit_bytes=60 * 2**20),
         )(*operands)
+        place = pl.BlockSpec(memory_space=pl.ANY)
+        return pl.pallas_call(
+            store,
+            out_shape=(jax.ShapeDtypeStruct((1, 1, block, width), F32),) * 2,
+            in_specs=[place] * 2,
+            out_specs=(place,) * 2,
+            scratch_shapes=[dma((2,))],
+        )(*results)
 
     return jax.shard_map(
         on_device,

time: 21.4 us -> 30.2 us (1.41)
  Pallas kernels: 18.7 us -> 27.4 us
    pallas_call x0 -> x1, Pallas kernels: none -> 9.06 us  [on_device(): pl.pallas_call(store, out_shape=(jax.ShapeDtypeStruct((1, 1, block, width...]
    unnamed x2 -> x4, local copies, waits for them, and re-layouts: 1.31 us -> 1.28 us
where the time goes in v5:
time: 30.2 us; the launch traced here: 30 us
  Pallas kernels  27.4 us (91%)
  between operations  1.3 us (4%)
  local copies, waits for them, and re-layouts  1.28 us (4%)
    pallas_call x1, Pallas kernels, on_device(): pl.pallas_call(functools.partial(kernel, rows, sectors, slices), out_shap...  18.4 us
    pallas_call x1, Pallas kernels, on_device(): pl.pallas_call(store, out_shape=(jax.ShapeDtypeStruct((1, 1, block, width...  9.06 us
    unnamed x4, local copies, waits for them, and re-layouts  1.28 us

profile of v5, /device:TPU:25, one launch (start us, length us, event | category | flops | bytes accessed | tf_op | source)
XLA Modules:
  0.0 30.0 jit_solution(16750939360220998102)
XLA Ops:
  1.3 18.4 %shard_map.86 = (f32[1,1,128,256]{3,2,1,0:T(8,128)S(1)}, f32[1,1,128,256]{3,2,1,0:T(8,128)S(1)}) custom-call(s32[1]{0:T(128)S(6)} %copy.9.ranks_hbm, s32[1,4]{1,0:T(1,128)} %routes_hbm.1, s32[8]{0:T(128)} %owner_hbm.1, f32[1,128,256]{2,1,0:T(8,128)} %boundary_hbm.1, f32[1,1,128,128]{3,2,1,0:T(8,128)} %left_hbm.1, f32[1,256,256]{2,1,0:T(8,128)} %right_hbm.1, ...), custom_call_target="tpu_custom_call" | custom-call | tf_op jit(solution)/shard_map/pallas_call | solution.py:263
  19.7 0.0 copy-start
  19.7 0.6 %copy-done = f32[1,1,128,256]{3,2,1,0:T(8,128)} copy-done((f32[1,1,128,256]{3,2,1,0:T(8,128)}, f32[1,1,128,256]{3,2,1,0:T(8,128)S(1)}, u32[]{:S(2)}) %copy-start) | copy-done | bytes 131096
  20.3 0.0 copy-start.1
  20.3 0.6 %copy-done.1 = f32[1,1,128,256]{3,2,1,0:T(8,128)} copy-done((f32[1,1,128,256]{3,2,1,0:T(8,128)}, f32[1,1,128,256]{3,2,1,0:T(8,128)S(1)}, u32[]{:S(2)}) %copy-start.1) | copy-done | bytes 131096
  21.0 9.1 %shard_map.87 = (f32[1,1,128,256]{3,2,1,0:T(8,128)}, f32[1,1,128,256]{3,2,1,0:T(8,128)}) custom-call(f32[1,1,128,256]{3,2,1,0:T(8,128)} %copy-done, f32[1,1,128,256]{3,2,1,0:T(8,128)} %copy-done.1), custom_call_target="tpu_custom_call" | custom-call | tf_op jit(solution)/shard_map/pallas_call | solution.py:293
Async XLA Ops:
  19.7 0.6 %copy-start = (f32[1,1,128,256]{3,2,1,0:T(8,128)}, f32[1,1,128,256]{3,2,1,0:T(8,128)S(1)}, u32[]{:S(2)}) copy-start(f32[1,1,128,256]{3,2,1,0:T(8,128)S(1)} %get-tuple-element.4.bound) | copy-start | bytes 393220
  20.3 0.6 %copy-start.1 = (f32[1,1,128,256]{3,2,1,0:T(8,128)}, f32[1,1,128,256]{3,2,1,0:T(8,128)S(1)}, u32[]{:S(2)}) copy-start(f32[1,1,128,256]{3,2,1,0:T(8,128)S(1)} %get-tuple-element.5.env) | copy-start | bytes 393220

commit v6 on v4

--- a/solution.py
+++ b/solution.py
@@ -121,20 +121,20 @@
         for step in range(1, slices):
             pair_copy(piece, step, group_base + partner(piece, step, slices)[0]).start()
 
+    for target in range(rows - 1, 0, -1):
+        @pl.when(row < target)
+        def _():
+            left_copy(row, target).start()
     pl.when(row == 0)(chain_step)
 
+    for step in range(1, sectors):
+        info_copy(sector, step, lax.rem(sector + step, sectors)).start()
     for step in range(groups - 1, 0, -1):
         start_copy(sector, start_send.at[step], partner(group, step, groups)[0] * 2 + core).start()
     start_copy(sector, start_send.at[0], twin).start()
-    for step in range(1, sectors):
-        info_copy(sector, step, lax.rem(sector + step, sectors)).start()
 
     pl.when((row > 0) & (row < rows - 1))(chain_step)
 
-    for target in range(rows - 1, 0, -1):
-        @pl.when(row < target)
-        def _():
-            left_copy(row, target).start()
     loads[6].wait()
     for step in range(1, sectors):
         source = lax.rem(sector + step, sectors)
@@ -191,9 +191,9 @@
         pair_copy(slot, step, group_base + slot).wait_recv()
     all_pairs = pairs[...].reshape(width, width)
     for source in range(sectors):
-        value = jnp.dot(starts[source], all_pairs, preferred_element_type=F32).astype(BF16)
-        moved[source] = value
-        terms[source] = jnp.dot(value, chosen[source], preferred_element_type=F32).astype(BF16)
+        moved[source] = jnp.dot(starts[source], all_pairs, preferred_element_type=F32).astype(BF16)
+    for source in range(sectors):
+        terms[source] = jnp.dot(moved[source], chosen[source], preferred_element_type=F32).astype(BF16)
 
     @pl.when(row == 0)
     def _():

time: 21.4 us -> 20.9 us (0.977)
  Pallas kernels: 18.7 us -> 18.1 us
    pallas_call x1, Pallas kernels: 18.7 us -> 18.1 us  [on_device(): pl.pallas_call(functools.partial(kernel, rows, sectors, slices), out_shap...]
where the time goes in v6:
time: 20.9 us; the launch traced here: 20.7 us
  Pallas kernels  18.1 us (87%)
  local copies, waits for them, and re-layouts  1.31 us (6%)
  between operations  1.29 us (6%)
    pallas_call x1, Pallas kernels, on_device(): pl.pallas_call(functools.partial(kernel, rows, sectors, slices), out_shap...  18.1 us
    unnamed x2, local copies, waits for them, and re-layouts  1.31 us

profile of v6, /device:TPU:25, one launch (start us, length us, event | category | flops | bytes accessed | tf_op | source)
XLA Modules:
  0.0 20.7 jit_solution(13174283292960548134)
XLA Ops:
  1.3 18.1 %shard_map.86 = (f32[1,1,128,256]{3,2,1,0:T(8,128)S(1)}, f32[1,1,128,256]{3,2,1,0:T(8,128)S(1)}) custom-call(s32[1]{0:T(128)S(6)} %copy.13.ranks_hbm, s32[1,4]{1,0:T(1,128)} %routes_hbm.1, s32[8]{0:T(128)} %owner_hbm.1, f32[1,128,256]{2,1,0:T(8,128)} %boundary_hbm.1, f32[1,1,128,128]{3,2,1,0:T(8,128)} %left_hbm.1, f32[1,256,256]{2,1,0:T(8,128)} %right_hbm.1, ...), custom_call_target="tpu_custom_call" | custom-call | tf_op jit(solution)/shard_map/pallas_call | solution.py:254
  19.4 0.7 %copy.11 = f32[1,1,128,256]{3,2,1,0:T(8,128)} copy(f32[1,1,128,256]{3,2,1,0:T(8,128)S(1)} %get-tuple-element.2) | data formatting | bytes 262144
  20.1 0.7 %copy.12 = f32[1,1,128,256]{3,2,1,0:T(8,128)} copy(f32[1,1,128,256]{3,2,1,0:T(8,128)S(1)} %get-tuple-element.3) | data formatting | bytes 262144

commit v7 on v6

--- a/solution.py
+++ b/solution.py
@@ -118,22 +118,28 @@
         @pl.when(row < rows - 1)
         def _():
             chain_copy().start()
+
+    def pair_step():
         for step in range(1, slices):
             pair_copy(piece, step, group_base + partner(piece, step, slices)[0]).start()
 
+    pl.when(row == 0)(chain_step)
+
     for target in range(rows - 1, 0, -1):
         @pl.when(row < target)
         def _():
             left_copy(row, target).start()
-    pl.when(row == 0)(chain_step)
-
     for step in range(1, sectors):
         info_copy(sector, step, lax.rem(sector + step, sectors)).start()
+    pl.when(row == 0)(pair_step)
     for step in range(groups - 1, 0, -1):
         start_copy(sector, start_send.at[step], partner(group, step, groups)[0] * 2 + core).start()
     start_copy(sector, start_send.at[0], twin).start()
 
-    pl.when((row > 0) & (row < rows - 1))(chain_step)
+    @pl.when((row > 0) & (row < rows - 1))
+    def _():
+        chain_step()
+        pair_step()
 
     loads[6].wait()
     for step in range(1, sectors):
@@ -169,7 +175,10 @@
             prefix_copy(sector, prefix_send.at[step], partner(group, step, groups)[0] * 2 + core).start()
         prefix_copy(sector, prefix_send.at[0], twin).start()
 
-    pl.when((row > 0) & (row == rows - 1))(chain_step)
+    @pl.when((row > 0) & (row == rows - 1))
+    def _():
+        chain_step()
+        pair_step()
 
     for step in range(groups - 1, 0, -1):
         slot = partner(group, step, groups)[1] * 2 + core

time: 20.9 us -> 20 us (0.957)
  Pallas kernels: 18.1 us -> 17.2 us
    pallas_call x1, Pallas kernels: 18.1 us -> 17.2 us  [on_device(): pl.pallas_call(functools.partial(kernel, rows, sectors, slices), out_shap...]
where the time goes in v7:
time: 20 us; the launch traced here: 19.8 us
  Pallas kernels  17.2 us (86%)
  local copies, waits for them, and re-layouts  1.31 us (7%)
  between operations  1.29 us (6%)
    pallas_call x1, Pallas kernels, on_device(): pl.pallas_call(functools.partial(kernel, rows, sectors, slices), out_shap...  17.2 us
    unnamed x2, local copies, waits for them, and re-layouts  1.31 us

profile of v7, /device:TPU:25, one launch (start us, length us, event | category | flops | bytes accessed | tf_op | source)
XLA Modules:
  0.0 19.8 jit_solution(16957570560251345348)
XLA Ops:
  1.3 17.2 %shard_map.86 = (f32[1,1,128,256]{3,2,1,0:T(8,128)S(1)}, f32[1,1,128,256]{3,2,1,0:T(8,128)S(1)}) custom-call(s32[1]{0:T(128)S(6)} %copy.13.ranks_hbm, s32[1,4]{1,0:T(1,128)} %routes_hbm.1, s32[8]{0:T(128)} %owner_hbm.1, f32[1,128,256]{2,1,0:T(8,128)} %boundary_hbm.1, f32[1,1,128,128]{3,2,1,0:T(8,128)} %left_hbm.1, f32[1,256,256]{2,1,0:T(8,128)} %right_hbm.1, ...), custom_call_target="tpu_custom_call" | custom-call | tf_op jit(solution)/shard_map/pallas_call | solution.py:263
  18.5 0.7 %copy.11 = f32[1,1,128,256]{3,2,1,0:T(8,128)} copy(f32[1,1,128,256]{3,2,1,0:T(8,128)S(1)} %get-tuple-element.2) | data formatting | bytes 262144
  19.2 0.7 %copy.12 = f32[1,1,128,256]{3,2,1,0:T(8,128)} copy(f32[1,1,128,256]{3,2,1,0:T(8,128)S(1)} %get-tuple-element.3) | data formatting | bytes 262144
